TPU v7x, 32 devices: a whole 2x2x4 slice. The times are simulated.
32 devices in a mesh: row: 8 (over z, core), col: 4 (over y, x).
Axes of the slice: x: 2, y: 2, z: 4, core: 2. Of those that a mesh axis runs over, the one named last changes fastest.
Arguments:
- loads: float32 [48, 1024, 4096], P(None, 'row', 'col'), may hold values from -6 to 6
- below_first: float32 [47, 1024, 1024], P(None, 'row', 'col'), may hold values from -0.1875 to 0.1875
- below_second: float32 [46, 1024, 1024], P(None, 'row', 'col'), may hold values from -0.1875 to 0.1875
- inverses: float32 [2, 1024, 1024], P(None, None, 'row'), may hold values from -1 to 2, as said below
Outputs:
- solved: float32 [2, 1024, 4096], P(None, None, 'col')
- remaining: float32 [46, 1024, 4096], P(None, 'row', 'col')
Inputs may be any that keep to these rules, and one draw needn't show every extreme that they name: `inverses`: each of the two matrices is lower triangular, with a diagonal from 0.5 to 2.
All inputs are finite; a program needn't handle non-finite values.
Results may differ from a plain program's by a relative error of at most 0.000084.
Values sent between devices are 32-bit elements; how exact they have to be, the bound alone decides.
A program may use at most 256 MiB of HBM per device.

v0:
```python
import jax
import jax.numpy as jnp
from jax import lax
from jax.sharding import PartitionSpec as P


def solve_block(inverse_part, block_rows):
    partial_value = jnp.dot(inverse_part, block_rows, precision=lax.Precision.HIGHEST)
    return lax.psum(partial_value, "row")


def strip_product(shard_piece, solution):
    columns = shard_piece.shape[2]
    flattened = shard_piece.reshape(-1, columns)
    return jnp.dot(flattened, solution, precision=lax.Precision.HIGHEST)


def local(loads, below_first, below_second, inverses):
    cycles, rows_dev, rhs_dev = loads.shape
    first_block = solve_block(inverses[0], loads[0])
    updated = loads[1:].reshape(-1, rhs_dev) - strip_product(
        lax.all_gather(below_first, "col", axis=2, tiled=True), first_block
    )
    updated = updated.reshape(cycles - 1, rows_dev, rhs_dev)
    second_block = solve_block(inverses[1], updated[0])
    remaining = updated[1:].reshape(-1, rhs_dev) - strip_product(
        lax.all_gather(below_second, "col", axis=2, tiled=True), second_block
    )
    solved = jnp.stack([first_block, second_block])
    return (solved, remaining.reshape(cycles - 2, rows_dev, rhs_dev))


def solution(mesh):
    in_specs = (
        P(None, "row", "col"),
        P(None, "row", "col"),
        P(None, "row", "col"),
        P(None, None, "row"),
    )
    out_specs = (P(None, None, "col"), P(None, "row", "col"))
    return jax.shard_map(local, mesh=mesh, in_specs=in_specs, out_specs=out_specs, check_vma=False)
```

profile of v0, /device:TPU:0, one launch (start us, length us, event | category | flops | bytes accessed | tf_op | source)
XLA Modules:
  0.0 741.3 jit_solution(17923245185394723700)
XLA Ops:
  8.0 0.0 all-reduce.3.cloned.1.call-start
  8.0 6.6 fusion.2
  14.7 0.0 all-reduce.3.cloned.1.call-update
  14.7 0.0 all-gather.3.cloned.1.call-start
  14.8 0.5 all-gather.3.cloned.1.call-update
  15.3 0.0 all-gather.5.cloned.1.call-start
  15.3 0.5 all-gather.5.cloned.1.call-update
  15.9 0.0 all-reduce.5.cloned.1.call-start
  15.9 19.4 %slice.22 = f32[47,128,1024]{2,1,0:T(8,128)} slice(f32[48,128,1024]{2,1,0:T(8,128)} %param.4), slice={[1:48], [0:128], [0:1024]} | slice | bytes 49283072 | tf_op jit(solution)/shard_map/slice | solution.py:21
  35.3 24.9 %copy.9 = f32[6016,1024]{0,1:T(8,128)} copy(f32[6016,1024]{1,0:T(8,128)} %bitcast.25) | data formatting | bytes 49283072 | tf_op jit(solution)/shard_map/reshape | solution.py:21
  60.3 53.8 %all-reduce.3.cloned.1.call-done = f32[1024,1024]{1,0:T(8,128)} async-done(((f32[1024,1024]{1,0:T(8,128)}), f32[1024,1024]{1,0:T(8,128)}) %all-reduce.3.cloned.1.call-update) | async-done | bytes 4194320 | tf_op jit(solution)/shard_map/psum | solution.py:9
  114.1 128.8 %all-gather.3.cloned.1.call-done = f32[47,128,1024]{2,1,0:T(8,128)} async-done(((f32[47,128,256]{2,1,0:T(8,128)}), f32[47,128,1024]{2,1,0:T(8,128)}) %all-gather.3.cloned.1.call-update) | async-done | bytes 24641552 | tf_op jit(solution)/shard_map/all_gather | solution.py:22
  242.8 0.0 copy-start
  242.8 178.1 %bitcast_subtract_fusion = f32[6016,1024]{0,1:T(8,128)} fusion(f32[6016,1024]{0,1:T(8,128)} %copy.9, f32[1024,1024]{1,0:T(8,128)} %all-reduce.3.cloned.1.call-done, f32[6016,1024]{1,0:T(8,128)} %bitcast.29), kind=kOutput, calls=%fused_computation | convolution fusion | flops 75704958976 | bytes 78118912 | tf_op jit(solution)/shard_map/dot_general | solution.py:15
  421.0 0.0 copy-done
  421.0 6.0 convolution_bitcast_fusion
  427.0 0.0 all-reduce.5.cloned.1.call-update
  427.0 36.3 %all-gather.5.cloned.1.call-done = f32[46,128,1024]{2,1,0:T(8,128)} async-done(((f32[46,128,256]{2,1,0:T(8,128)}), f32[46,128,1024]{2,1,0:T(8,128)}) %all-gather.5.cloned.1.call-update) | async-done | bytes 24117264 | tf_op jit(solution)/shard_map/all_gather | solution.py:27
  463.4 60.8 %all-reduce.5.cloned.1.call-done = f32[1024,1024]{1,0:T(8,128)} async-done(((f32[1024,1024]{1,0:T(8,128)}), f32[1024,1024]{1,0:T(8,128)}) %all-reduce.5.cloned.1.call-update) | async-done | bytes 4194320 | tf_op jit(solution)/shard_map/psum | solution.py:9
  524.1 176.9 %slice_subtract_fusion = f32[5888,1024]{0,1:T(8,128)} fusion(f32[6016,1024]{0,1:T(8,128)} %bitcast_subtract_fusion, f32[1024,1024]{1,0:T(8,128)} %all-reduce.5.cloned.1.call-done, f32[5888,1024]{1,0:T(8,128)} %bitcast.30), kind=kOutput, calls=%fused_computation.1 | convolution fusion | flops 74094215168 | bytes 76546048 | tf_op jit(solution)/shard_map/dot_general | solution.py:15
  701.0 24.1 %copy.11 = f32[5888,1024]{1,0:T(8,128)} copy(f32[5888,1024]{0,1:T(8,128)} %slice_subtract_fusion) | data formatting | bytes 48234496 | tf_op jit(solution)/shard_map/sub | solution.py:26
  725.1 8.5 %pad_maximum_fusion = f32[2,1024,1024]{2,1,0:T(8,128)} fusion(f32[1,1024,1024]{2,1,0:T(8,128)} %bitcast.28, f32[1,1024,1024]{2,1,0:T(8,128)} %bitcast.27), kind=kLoop, calls=%fused_computation.2 | loop fusion | flops 2097152 | bytes 16777216 | tf_op jit(solution)/shard_map/stack | solution.py:29
Async XLA Ops:
  8.0 106.1 %all-reduce.3.cloned.1.call-start = ((), (), s32[]{:S(2)}) async-start(), calls=%async_computation | async-start | bytes 8388608 | tf_op jit(solution)/shard_map/psum | solution.py:9
  14.7 228.1 %all-gather.3.cloned.1.call-start = ((), (), s32[]{:S(2)}) async-start(), calls=%async_computation.1 | async-start | bytes 30801920 | tf_op jit(solution)/shard_map/all_gather | solution.py:22
  15.3 448.1 %all-gather.5.cloned.1.call-start = ((), (), s32[]{:S(2)}) async-start(), calls=%async_computation.3 | async-start | bytes 30146560 | tf_op jit(solution)/shard_map/all_gather | solution.py:27
  15.9 508.3 %all-reduce.5.cloned.1.call-start = ((), (), s32[]{:S(2)}) async-start(), calls=%async_computation.2 | async-start | bytes 8388608 | tf_op jit(solution)/shard_map/psum | solution.py:9
  242.8 178.1 %copy-start = (f32[2,1024,128]{2,1,0:T(8,128)S(1)}, f32[2,1024,128]{2,1,0:T(8,128)}, u32[]{:S(2)}) copy-start(f32[2,1024,128]{2,1,0:T(8,128)} %param.7) | copy-start | bytes 3145732
Sparse Core Ops, SparseCore 0:
  14.8 99.2 all-reduce.2
  427.1 96.9 all-reduce.4
Sparse Core Ops, SparseCore 1:
  17.0 225.8 all-gather.2
  244.6 218.7 all-gather.4
where the time goes:
time: 746 us; the launch traced here: 741 us
  matrix products  368 us (49%)
  waiting for transfers between devices  281 us (38%)
  local copies, waits for them, and re-layouts  68.4 us (9%)
  between operations  15.7 us (2%)
  other arithmetic  8.53 us (1%)
    dot_general x2, matrix products, strip_product(): return jnp.dot(flattened, solution, precision=lax.Precision.HIGHEST)  355 us
    all_gather x1, waiting for transfers between devices, local(): lax.all_gather(below_first, 'col', axis=2, tiled=True)  129 us
    psum x2, waiting for transfers between devices, solve_block(): return lax.psum(partial_value, 'row')  115 us
    all_gather x1, waiting for transfers between devices, local(): lax.all_gather(below_second, 'col', axis=2, tiled=True)  36.3 us
    reshape x1, local copies, waits for them, and re-layouts, local(): loads[1:].reshape(-1, rhs_dev)  24.9 us
    sub x1, local copies, waits for them, and re-layouts, local(): updated[1:].reshape(-1, rhs_dev)  24.1 us
    slice x1, local copies, waits for them, and re-layouts, local(): loads[1:].reshape(-1, rhs_dev)  19.4 us
  transfers between devices with their start and end apart: 4, of which 4 were waited for; matrix products, arithmetic and copies ran while one was open for 31% of the time, Pallas kernels for 0%

commit v1 on v0

v1 whole, which is shorter than its diff:
```python
import functools
import jax
import jax.numpy as jnp
from jax import lax
from jax.experimental import pallas as pl
from jax.experimental.pallas import tpu as pltpu
from jax.sharding import PartitionSpec as P

HIGH = lax.Precision.HIGH
STEP = 4


def chunk_sizes(count):
    tail = count % STEP
    steps = count // STEP
    sizes = []
    for share in (4, 3, 3):
        now = min(-(-steps * share // 11), steps - sum(sizes))
        if now > 0:
            sizes.append(now)
    if steps > sum(sizes):
        sizes.append(steps - sum(sizes))
    return [size * STEP for size in sizes] + ([tail] if tail else [])


def halves(value):
    high = lax.reduce_precision(value, 8, 7)
    return high.astype(jnp.bfloat16), (value - high).astype(jnp.bfloat16)


def update_kernel(step, a1, a2, *refs):
    loads = refs[:step // 2]
    f1h, f1l, f2h, f2l = refs[step // 2:step // 2 + 4]
    out = refs[-1]
    rows = a1.shape[1]
    total = None
    for a, fh, fl in ((a1, f1h, f1l), (a2, f2h, f2l)):
        whole = a[...].reshape(step * rows, a.shape[2])
        high = whole.astype(jnp.bfloat16)
        low = (whole - high.astype(jnp.float32)).astype(jnp.bfloat16)
        for x, y in ((high, fh), (high, fl), (low, fh)):
            term = jnp.dot(x, y[...], preferred_element_type=jnp.float32)
            total = term if total is None else total + term
    total = total.reshape(step, rows, total.shape[1])
    for at, part in enumerate(loads):
        out[2 * at:2 * at + 2] = part[...] - total[2 * at:2 * at + 2]


def update_chunk(a1, a2, loads, factors, offset, previous):
    size, rows, depth = a1.shape
    columns = loads.shape[2]
    count = loads.shape[0] - 2
    step = STEP if size % STEP == 0 else 2
    pairs = step // 2
    block = pl.BlockSpec((step, rows, depth), lambda i: (i, 0, 0))
    load_specs = [
        pl.BlockSpec((2, rows, columns), lambda i, k=k: (1 + offset // 2 + i * pairs + k, 0, 0))
        for k in range(pairs)
    ]
    full = pl.BlockSpec((depth, columns), lambda i: (0, 0), pipeline_mode=pl.Buffered(1))
    operands = [a1, a2] + [loads] * pairs + list(factors)
    in_specs = [block, block] + load_specs + [full] * 4
    aliases = {}
    if previous is not None:
        aliases = {len(operands): 0}
        operands.append(previous)
        in_specs.append(pl.BlockSpec(memory_space=pl.ANY))
    work = size * rows * depth * columns
    return pl.pallas_call(
        functools.partial(update_kernel, step),
        out_shape=jax.ShapeDtypeStruct((count, rows, columns), jnp.float32),
        grid=(size // step,),
        in_specs=in_specs,
        out_specs=pl.BlockSpec((step, rows, columns), lambda i: (offset // step + i, 0, 0)),
        input_output_aliases=aliases,
        compiler_params=pltpu.CompilerParams(vmem_limit_bytes=48 * 1024 * 1024),
        cost_estimate=pl.CostEstimate(
            flops=12 * work,
            bytes_accessed=8 * size * rows * (depth + columns) + 8 * depth * columns,
            transcendentals=0,
        ),
    )(*operands)


def local(loads, below_first, below_second, inverses):
    cycles = loads.shape[0]
    gather = lambda piece: lax.all_gather(piece, "col", axis=2, tiled=True)
    slices = []
    at = 0
    for size in chunk_sizes(cycles - 2):
        slices.append([below_first[at + 1:at + 1 + size], below_second[at:at + size], at])
        at += size
    top = gather(below_first[:1])
    early = [gather(piece) for piece in slices[0][:2]]
    first_block = lax.psum(jnp.dot(inverses[0], loads[0], precision=HIGH), "row")
    later = [piece[:2] for piece in slices[1:]]
    first_block, later = lax.optimization_barrier((first_block, later))
    updated = loads[1] - jnp.dot(top[0], first_block, precision=HIGH)
    updated, early = lax.optimization_barrier((updated, early))
    second_block = lax.psum(jnp.dot(inverses[1], updated, precision=HIGH), "row")
    factors = halves(first_block) + halves(second_block)
    pieces = [early] + [[gather(piece) for piece in pair] for pair in later]
    remaining = None
    for (a1, a2), (_, _, offset) in zip(pieces, slices):
        remaining = update_chunk(a1, a2, loads, factors, offset, remaining)
    return (jnp.stack([first_block, second_block]), remaining)


def solution(mesh):
    in_specs = (
        P(None, "row", "col"),
        P(None, "row", "col"),
        P(None, "row", "col"),
        P(None, None, "row"),
    )
    out_specs = (P(None, None, "col"), P(None, "row", "col"))
    return jax.shard_map(local, mesh=mesh, in_specs=in_specs, out_specs=out_specs, check_vma=False)
```

time: 746 us -> 639 us (0.86)
  matrix products: 368 us -> 14.4 us
  waiting for transfers between devices: 281 us -> 440 us
  Pallas kernels: 0 us -> 105 us
  local copies, waits for them, and re-layouts: 68.4 us -> 30.3 us
  blocking collectives: 0 us -> 17 us
    dot_general x4 -> x3, matrix products: 368 us -> 14.4 us  [the longest x1 5.61 us: local(): updated = loads[1] - jnp.dot(top[0], first_block, precision=HIGH)]
    all_gather x2 -> x10, waiting for transfers between devices: 165 us -> 288 us  [local(): gather = lambda piece: lax.all_gather(piece, 'col', axis=2, tiled=True)]
    pallas_call x0 -> x5, Pallas kernels: none -> 105 us  [update_chunk(): pl.pallas_call(functools.partial(update_kernel, step), out_shape=jax.Shap...]
    psum x2, waiting for transfers between devices: 115 us -> 148 us  [the longest x1 87.1 us: local(): lax.psum(jnp.dot(inverses[1], updated, precision=HIGH), 'row')]
    reshape x1 -> x0, local copies, waits for them, and re-layouts: 24.9 us -> none  [local(): loads[1:].reshape(-1, rhs_dev)]
    sub x1 -> x0, local copies, waits for them, and re-layouts: 24.1 us -> none  [local(): updated[1:].reshape(-1, rhs_dev)]
    all_gather x0 -> x1, blocking collectives: none -> 17 us  [local(): gather = lambda piece: lax.all_gather(piece, 'col', axis=2, tiled=True)]
    convert_element_type x0 -> x2, other arithmetic: none -> 10 us  [halves(): return (high.astype(jnp.bfloat16), (value - high).astype(jnp.bfloat16))]
  transfers between devices with their start and end apart: 4 -> 12, of which waited for: 4 -> 10; matrix products, arithmetic and copies ran while one was open for 31% -> 7% of each run, Pallas kernels for 0% -> 15%
where the time goes in v1:
time: 639 us; the launch traced here: 638 us
  waiting for transfers between devices  440 us (69%)
  Pallas kernels  105 us (16%)
  local copies, waits for them, and re-layouts  30.3 us (5%)
  blocking collectives  17 us (3%)
  between operations  15.7 us (2%)
  other arithmetic  15.1 us (2%)
  matrix products  14.4 us (2%)
    all_gather x10, waiting for transfers between devices, local(): gather = lambda piece: lax.all_gather(piece, 'col', axis=2, tiled=True)  288 us
    pallas_call x5, Pallas kernels, update_chunk(): pl.pallas_call(functools.partial(update_kernel, step), out_shape=jax.Shap...  105 us
    psum x1, waiting for transfers between devices, local(): lax.psum(jnp.dot(inverses[1], updated, precision=HIGH), 'row')  87.1 us
    psum x1, waiting for transfers between devices, local(): lax.psum(jnp.dot(inverses[0], loads[0], precision=HIGH), 'row')  60.7 us
    all_gather x1, blocking collectives, local(): gather = lambda piece: lax.all_gather(piece, 'col', axis=2, tiled=True)  17 us
  transfers between devices with their start and end apart: 12, of which 10 were waited for; matrix products, arithmetic and copies ran while one was open for 7% of the time, Pallas kernels for 15%

profile of v1, /device:TPU:0, one launch (start us, length us, event | category | flops | bytes accessed | tf_op | source)
XLA Modules:
  0.0 637.9 jit_solution(738882460424479055)
XLA Ops:
  8.0 5.0 fusion.5
  26.9 17.0 %all_gather.33 = f32[1,128,1024]{2,1,0:T(8,128)S(1)} all-gather(f32[1,128,256]{2,1,0:T(8,128)S(1)} %slice-done.1), channel_id=1, replica_groups=mesh['row'=8,'col'=4] {'col'}, dimensions={2}, use_global_device_ids=true | all-gather | bytes 655360 | tf_op jit(solution)/shard_map/all_gather | solution.py:87
  43.9 3.9 fusion.11
  47.8 3.9 fusion.12
  51.7 60.7 %all-reduce.3.cloned.1.call-done = f32[1024,1024]{1,0:T(8,128)} async-done(((f32[1024,1024]{1,0:T(8,128)}), f32[1024,1024]{1,0:T(8,128)}) %all-reduce.3.cloned.1.call-update) | async-done | bytes 4194320 | tf_op jit(solution)/shard_map/psum | solution.py:95
  112.4 5.6 fusion.2
  118.1 81.5 %all-gather.13.cloned.1.call-done.a2 = f32[16,128,1024]{2,1,0:T(8,128)} async-done(((f32[16,128,256]{2,1,0:T(8,128)}), f32[16,128,1024]{2,1,0:T(8,128)}) %all-gather.13.cloned.1.call-update) | async-done | bytes 8388624 | tf_op jit(solution)/shard_map/all_gather | solution.py:87
  199.6 3.8 convolution_bitcast_fusion
  208.2 4.7 fusion
  213.0 87.1 %all-reduce.5.cloned.1.call-done = f32[1024,1024]{1,0:T(8,128)} async-done(((f32[1024,1024]{1,0:T(8,128)}), f32[1024,1024]{1,0:T(8,128)}) %all-reduce.5.cloned.1.call-update) | async-done | bytes 4194320 | tf_op jit(solution)/shard_map/psum | solution.py:100
  300.1 5.3 fusion.1
  305.4 32.8 %shard_map.59.refs_6_ = f32[46,128,1024]{2,1,0:T(8,128)} custom-call(f32[16,128,1024]{2,1,0:T(8,128)} %all-gather.11.cloned.1.call-done.a1, f32[16,128,1024]{2,1,0:T(8,128)} %all-gather.13.cloned.1.call-done.a2, f32[48,128,1024]{2,1,0:T(8,128)} %refs_0_.9, f32[48,128,1024]{2,1,0:T(8,128)} %refs_0_.9, bf16[1024,1024]{1,0:T(8,128)(2,1)S(1)} %copy-done.1, ...), custom_call_target="tpu_custom_call" | custom-call | flops 25769803776 | bytes 41943040 | tf_op jit(solution)/shard_map/pallas_call | solution.py:69
  338.2 9.2 %all-gather.29.cloned.1.call-done.a2 = f32[12,128,1024]{2,1,0:T(8,128)} async-done(((f32[12,128,256]{2,1,0:T(8,128)}), f32[12,128,1024]{2,1,0:T(8,128)}) %all-gather.29.cloned.1.call-update) | async-done | bytes 6291472 | tf_op jit(solution)/shard_map/all_gather | solution.py:87
  348.9 26.1 %shard_map.60.refs_6_ = f32[46,128,1024]{2,1,0:T(8,128)} custom-call(f32[12,128,1024]{2,1,0:T(8,128)} %all-gather.27.cloned.1.call-done.a1, f32[12,128,1024]{2,1,0:T(8,128)} %all-gather.29.cloned.1.call-done.a2, f32[48,128,1024]{2,1,0:T(8,128)} %refs_0_.9, f32[48,128,1024]{2,1,0:T(8,128)} %refs_0_.9, ...), custom_call_target="tpu_custom_call", output_to_operand_aliasing={{}: (8, {})} | custom-call | flops 19327352832 | bytes 33554432 | tf_op jit(solution)/shard_map/pallas_call | solution.py:69
  375.0 44.1 %all-gather.23.cloned.1.call-done.a1 = f32[12,128,1024]{2,1,0:T(8,128)} async-done(((f32[12,128,256]{2,1,0:T(8,128)}), f32[12,128,1024]{2,1,0:T(8,128)}) %all-gather.23.cloned.1.call-update) | async-done | bytes 6291472 | tf_op jit(solution)/shard_map/all_gather | solution.py:87
  419.1 71.7 %all-gather.25.cloned.1.call-done.a2 = f32[12,128,1024]{2,1,0:T(8,128)} async-done(((f32[12,128,256]{2,1,0:T(8,128)}), f32[12,128,1024]{2,1,0:T(8,128)}) %all-gather.25.cloned.1.call-update) | async-done | bytes 6291472 | tf_op jit(solution)/shard_map/all_gather | solution.py:87
  492.4 26.4 %shard_map.61.refs_6_ = f32[46,128,1024]{2,1,0:T(8,128)} custom-call(f32[12,128,1024]{2,1,0:T(8,128)} %all-gather.23.cloned.1.call-done.a1, f32[12,128,1024]{2,1,0:T(8,128)} %all-gather.25.cloned.1.call-done.a2, f32[48,128,1024]{2,1,0:T(8,128)} %refs_0_.9, f32[48,128,1024]{2,1,0:T(8,128)} %refs_0_.9, ...), custom_call_target="tpu_custom_call", output_to_operand_aliasing={{}: (8, {})} | custom-call | flops 19327352832 | bytes 33554432 | tf_op jit(solution)/shard_map/pallas_call | solution.py:69
  518.8 5.1 pad_maximum_fusion
  523.9 3.6 all-gather.19.cloned.1.call-done.a1
  527.5 36.7 %all-gather.21.cloned.1.call-done.a2 = f32[4,128,1024]{2,1,0:T(8,128)} async-done(((f32[4,128,256]{2,1,0:T(8,128)}), f32[4,128,1024]{2,1,0:T(8,128)}) %all-gather.21.cloned.1.call-update) | async-done | bytes 2097168 | tf_op jit(solution)/shard_map/all_gather | solution.py:87
  567.4 12.0 %shard_map.62.refs_5_ = f32[46,128,1024]{2,1,0:T(8,128)} custom-call(f32[4,128,1024]{2,1,0:T(8,128)S(1)} %copy-done.5, f32[4,128,1024]{2,1,0:T(8,128)S(1)} %copy-done.6, f32[48,128,1024]{2,1,0:T(8,128)} %refs_0_.9, f32[48,128,1024]{2,1,0:T(8,128)} %refs_0_.9, bf16[1024,1024]{1,0:T(8,128)(2,1)} %get-tuple-element.33.refs_2_.refs_1_, ...), custom_call_target="tpu_custom_call", output_to_operand_aliasing={{}: (8, {})} | custom-call | flops 6442450944 | bytes 16777216 | tf_op jit(solution)/shard_map/pallas_call | solution.py:69
  579.5 12.8 %all-gather.15.cloned.1.call-done.a1 = f32[2,128,1024]{2,1,0:T(8,128)} async-done(((f32[2,128,256]{2,1,0:T(8,128)}), f32[2,128,1024]{2,1,0:T(8,128)}) %all-gather.15.cloned.1.call-update) | async-done | bytes 1048592 | tf_op jit(solution)/shard_map/all_gather | solution.py:87
  592.3 28.2 %all-gather.17.cloned.1.call-done.a2 = f32[2,128,1024]{2,1,0:T(8,128)} async-done(((f32[2,128,256]{2,1,0:T(8,128)}), f32[2,128,1024]{2,1,0:T(8,128)}) %all-gather.17.cloned.1.call-update) | async-done | bytes 1048592 | tf_op jit(solution)/shard_map/all_gather | solution.py:87
  622.9 7.5 %shard_map.63 = f32[46,128,1024]{2,1,0:T(8,128)} custom-call(f32[2,128,1024]{2,1,0:T(8,128)S(1)} %copy-done.7, f32[2,128,1024]{2,1,0:T(8,128)S(1)} %copy-done.8, f32[48,128,1024]{2,1,0:T(8,128)} %refs_0_.9, bf16[1024,1024]{1,0:T(8,128)(2,1)S(1)} %copy-done.4, bf16[1024,1024]{1,0:T(8,128)(2,1)} %copy-done, ...), custom_call_target="tpu_custom_call", output_to_operand_aliasing={{}: (7, {})} | custom-call | flops 3221225472 | bytes 12582912 | tf_op jit(solution)/shard_map/pallas_call | solution.py:69
  (61 shorter events, 27.4 us)
Async XLA Ops:
  8.0 104.4 %all-reduce.3.cloned.1.call-start = ((), (), s32[]{:S(2)}) async-start(), calls=%async_computation | async-start | bytes 8388608 | tf_op jit(solution)/shard_map/psum | solution.py:95
  13.1 105.0 %all-gather.11.cloned.1.call-start = ((), (), s32[]{:S(2)}) async-start(), calls=%async_computation.1 | async-start | bytes 10485760 | tf_op jit(solution)/shard_map/all_gather | solution.py:87
  16.2 183.3 %all-gather.13.cloned.1.call-start = ((), (), s32[]{:S(2)}) async-start(), calls=%async_computation.2 | async-start | bytes 10485760 | tf_op jit(solution)/shard_map/all_gather | solution.py:87
  19.4 7.3 %slice-start = ((f32[48,128,1024]{2,1,0:T(8,128)}), f32[1,128,1024]{2,1,0:T(8,128)S(1)}, s32[]{:S(2)}) async-start(f32[48,128,1024]{2,1,0:T(8,128)} %refs_0_.9), calls=%async_computation.12 | async-start | bytes 1048576 | tf_op jit(solution)/shard_map/slice | solution.py:98
  19.4 7.5 %slice-start.1 = ((f32[47,128,256]{2,1,0:T(8,128)}), f32[1,128,256]{2,1,0:T(8,128)S(1)}, s32[]{:S(2)}) async-start(f32[47,128,256]{2,1,0:T(8,128)} %param.5), calls=%async_computation.13 | async-start | bytes 262144 | tf_op jit(solution)/shard_map/slice | solution.py:93
  19.4 280.7 %all-reduce.5.cloned.1.call-start = ((), (), s32[]{:S(2)}) async-start(), calls=%async_computation.3 | async-start | bytes 8388608 | tf_op jit(solution)/shard_map/psum | solution.py:100
  51.7 147.9 %copy-start.11 = (f32[2,1024,128]{2,1,0:T(8,128)S(1)}, f32[2,1024,128]{2,1,0:T(8,128)}, u32[]{:S(2)}) copy-start(f32[2,1024,128]{2,1,0:T(8,128)} %param.7) | copy-start | bytes 3145732
  203.4 134.7 %all-gather.27.cloned.1.call-start = ((), (), s32[]{:S(2)}) async-start(), calls=%async_computation.10 | async-start | bytes 7864320 | tf_op jit(solution)/shard_map/all_gather | solution.py:87
  204.0 143.3 %all-gather.29.cloned.1.call-start = ((), (), s32[]{:S(2)}) async-start(), calls=%async_computation.11 | async-start | bytes 7864320 | tf_op jit(solution)/shard_map/all_gather | solution.py:87
  204.7 214.3 %all-gather.23.cloned.1.call-start = ((), (), s32[]{:S(2)}) async-start(), calls=%async_computation.8 | async-start | bytes 7864320 | tf_op jit(solution)/shard_map/all_gather | solution.py:87
  205.5 285.3 %all-gather.25.cloned.1.call-start = ((), (), s32[]{:S(2)}) async-start(), calls=%async_computation.9 | async-start | bytes 7864320 | tf_op jit(solution)/shard_map/all_gather | solution.py:87
  206.2 321.3 %all-gather.19.cloned.1.call-start = ((), (), s32[]{:S(2)}) async-start(), calls=%async_computation.6 | async-start | bytes 2621440 | tf_op jit(solution)/shard_map/all_gather | solution.py:87
  206.8 357.4 %all-gather.21.cloned.1.call-start = ((), (), s32[]{:S(2)}) async-start(), calls=%async_computation.7 | async-start | bytes 2621440 | tf_op jit(solution)/shard_map/all_gather | solution.py:87
  207.4 384.9 %all-gather.15.cloned.1.call-start = ((), (), s32[]{:S(2)}) async-start(), calls=%async_computation.4 | async-start | bytes 1310720 | tf_op jit(solution)/shard_map/all_gather | solution.py:87
  208.0 412.5 %all-gather.17.cloned.1.call-start = ((), (), s32[]{:S(2)}) async-start(), calls=%async_computation.5 | async-start | bytes 1310720 | tf_op jit(solution)/shard_map/all_gather | solution.py:87
  213.0 277.8 %copy-start = (bf16[1024,1024]{1,0:T(8,128)(2,1)}, bf16[1024,1024]{1,0:T(8,128)(2,1)S(1)}, u32[]{:S(2)}) copy-start(bf16[1024,1024]{1,0:T(8,128)(2,1)S(1)} %get-tuple-element.32.refs_3_.refs_2_) | copy-start | bytes 6291460
  300.1 5.3 copy-start.1
  347.3 1.6 copy-start.2
  490.8 1.6 copy-start.3
  492.4 26.4 %copy-start.9 = (f32[1024,1024]{1,0:T(8,128)S(1)}, f32[1024,1024]{1,0:T(8,128)}, u32[]{:S(2)}) copy-start(f32[1024,1024]{1,0:T(8,128)} %all-reduce.3.cloned.1.call-done) | copy-start | bytes 12582916
  492.4 26.4 %copy-start.10 = (f32[1024,1024]{1,0:T(8,128)S(1)}, f32[1024,1024]{1,0:T(8,128)}, u32[]{:S(2)}) copy-start(f32[1024,1024]{1,0:T(8,128)} %all-reduce.5.cloned.1.call-done) | copy-start | bytes 12582916
  523.9 96.6 %copy-start.4 = (bf16[1024,1024]{1,0:T(8,128)(2,1)S(1)}, bf16[1024,1024]{1,0:T(8,128)(2,1)}, u32[]{:S(2)}) copy-start(bf16[1024,1024]{1,0:T(8,128)(2,1)} %get-tuple-element.33.refs_2_.refs_1_) | copy-start | bytes 6291460
  564.2 1.6 copy-start.5
  565.8 1.6 copy-start.6
  (2 other events, 2.5 us)
Sparse Core Ops, SparseCore 0:
  13.2 99.2 all-reduce.2
  203.5 96.5 all-reduce.4
Sparse Core Ops, SparseCore 1:
  16.3 94.2 all-gather.10
  112.3 87.3 all-gather.12
  205.7 69.8 all-gather.26
  277.5 69.8 all-gather.28
  349.2 69.8 all-gather.22
  420.9 69.8 all-gather.24
  492.5 35.0 all-gather.18
  529.2 35.0 all-gather.20
  565.9 26.3 all-gather.14
  594.1 26.3 all-gather.16

commit v2 on v1

--- a/solution.py
+++ b/solution.py
@@ -11,16 +11,9 @@
 
 
 def chunk_sizes(count):
-    tail = count % STEP
-    steps = count // STEP
-    sizes = []
-    for share in (4, 3, 3):
-        now = min(-(-steps * share // 11), steps - sum(sizes))
-        if now > 0:
-            sizes.append(now)
-    if steps > sum(sizes):
-        sizes.append(steps - sum(sizes))
-    return [size * STEP for size in sizes] + ([tail] if tail else [])
+    last = 4
+    middle = count * 2 // 5 // 2 * 2
+    return [count - middle - last, middle, last]
 
 
 def halves(value):
@@ -46,20 +39,22 @@
         out[2 * at:2 * at + 2] = part[...] - total[2 * at:2 * at + 2]
 
 
-def update_chunk(a1, a2, loads, factors, offset, previous):
-    size, rows, depth = a1.shape
+def update_chunk(both, loads, factors, offset, previous):
+    rows, depth = both.shape[1:]
+    size = both.shape[0] // 2
     columns = loads.shape[2]
     count = loads.shape[0] - 2
-    step = STEP if size % STEP == 0 else 2
+    step = STEP if size % STEP == 0 and offset % STEP == 0 else 2
     pairs = step // 2
     block = pl.BlockSpec((step, rows, depth), lambda i: (i, 0, 0))
+    block2 = pl.BlockSpec((step, rows, depth), lambda i: (size // step + i, 0, 0))
     load_specs = [
         pl.BlockSpec((2, rows, columns), lambda i, k=k: (1 + offset // 2 + i * pairs + k, 0, 0))
         for k in range(pairs)
     ]
     full = pl.BlockSpec((depth, columns), lambda i: (0, 0), pipeline_mode=pl.Buffered(1))
-    operands = [a1, a2] + [loads] * pairs + list(factors)
-    in_specs = [block, block] + load_specs + [full] * 4
+    operands = [both, both] + [loads] * pairs + list(factors)
+    in_specs = [block, block2] + load_specs + [full] * 4
     aliases = {}
     if previous is not None:
         aliases = {len(operands): 0}
@@ -85,24 +80,25 @@
 def local(loads, below_first, below_second, inverses):
     cycles = loads.shape[0]
     gather = lambda piece: lax.all_gather(piece, "col", axis=2, tiled=True)
-    slices = []
+    chunks, offsets = [], []
     at = 0
     for size in chunk_sizes(cycles - 2):
-        slices.append([below_first[at + 1:at + 1 + size], below_second[at:at + size], at])
+        chunks.append(jnp.concatenate([below_first[at + 1:at + 1 + size], below_second[at:at + size]]))
+        offsets.append(at)
         at += size
+    inverses, chunks[0] = lax.optimization_barrier((inverses, chunks[0]))
+    early = gather(chunks[0])
     top = gather(below_first[:1])
-    early = [gather(piece) for piece in slices[0][:2]]
     first_block = lax.psum(jnp.dot(inverses[0], loads[0], precision=HIGH), "row")
-    later = [piece[:2] for piece in slices[1:]]
-    first_block, later = lax.optimization_barrier((first_block, later))
+    first_block, later = lax.optimization_barrier((first_block, chunks[1:]))
     updated = loads[1] - jnp.dot(top[0], first_block, precision=HIGH)
-    updated, early = lax.optimization_barrier((updated, early))
-    second_block = lax.psum(jnp.dot(inverses[1], updated, precision=HIGH), "row")
+    terms = jnp.dot(inverses[1], updated, precision=HIGH)
+    terms, early = lax.optimization_barrier((terms, early))
+    second_block = lax.psum(terms, "row")
     factors = halves(first_block) + halves(second_block)
-    pieces = [early] + [[gather(piece) for piece in pair] for pair in later]
     remaining = None
-    for (a1, a2), (_, _, offset) in zip(pieces, slices):
-        remaining = update_chunk(a1, a2, loads, factors, offset, remaining)
+    for both, offset in zip([early] + [gather(chunk) for chunk in later], offsets):
+        remaining = update_chunk(both, loads, factors, offset, remaining)
     return (jnp.stack([first_block, second_block]), remaining)
 
 

time: 639 us -> 505 us (0.79)
  waiting for transfers between devices: 440 us -> 336 us
  local copies, waits for them, and re-layouts: 30.3 us -> 9.55 us
  Pallas kernels: 105 us -> 93.2 us
  other arithmetic: 15.1 us -> 25.8 us
    all_gather x10 -> x3, waiting for transfers between devices: 288 us -> 166 us  [local(): gather = lambda piece: lax.all_gather(piece, 'col', axis=2, tiled=True)]
    psum x1, waiting for transfers between devices: 60.7 us -> 77.4 us  [local(): lax.psum(jnp.dot(inverses[0], loads[0], precision=HIGH), 'row')]
    pallas_call x5 -> x3, Pallas kernels: 105 us -> 93.2 us  [update_chunk(): pl.pallas_call(functools.partial(update_kernel, step), out_shape=jax.Shap...]
    concatenate x0 -> x3, other arithmetic: none -> 9.44 us  [local(): jnp.concatenate([below_first[at + 1:at + 1 + size], below_second[at:at +...]
    slice x4 -> x6, local copies, waits for them, and re-layouts: 10.6 us -> 1.88 us  [local(): below_first[at + 1:at + 1 + size]]
  transfers between devices with their start and end apart: 12 -> 5, of which waited for: 10 -> 5; matrix products, arithmetic and copies ran while one was open for 7% -> 7% of each run, Pallas kernels for 15% -> 16%
where the time goes in v2:
time: 505 us
  waiting for transfers between devices  336 us (67%)
  Pallas kernels  93.2 us (18%)
  other arithmetic  25.8 us (5%)
  between operations  15.7 us (3%)
  matrix products  12.5 us (2%)
  blocking collectives  11.5 us (2%)
  local copies, waits for them, and re-layouts  9.55 us (2%)
    all_gather x3, waiting for transfers between devices, local(): gather = lambda piece: lax.all_gather(piece, 'col', axis=2, tiled=True)  166 us
    pallas_call x3, Pallas kernels, update_chunk(): pl.pallas_call(functools.partial(update_kernel, step), out_shape=jax.Shap...  93.2 us
    psum x1, waiting for transfers between devices, local(): second_block = lax.psum(terms, 'row')  91.5 us
    psum x1, waiting for transfers between devices, local(): lax.psum(jnp.dot(inverses[0], loads[0], precision=HIGH), 'row')  77.4 us
    all_gather x1, blocking collectives, local(): gather = lambda piece: lax.all_gather(piece, 'col', axis=2, tiled=True)  11.5 us
  transfers between devices with their start and end apart: 5, of which 5 were waited for; matrix products, arithmetic and copies ran while one was open for 7% of the time, Pallas kernels for 16%

profile of v2, /device:TPU:0, one launch (start us, length us, event | category | flops | bytes accessed | tf_op | source)
XLA Modules:
  0.0 504.7 jit_solution(5230112477139280542)
XLA Ops:
  8.1 1.9 slice-done
  9.9 1.0 slice-done.4
  10.9 3.2 pad_maximum_fusion.1
  14.1 5.0 fusion.6
  19.8 3.5 slice.38
  23.3 11.5 %all_gather.12 = f32[1,128,1024]{2,1,0:T(8,128)S(1)} all-gather(f32[1,128,256]{2,1,0:T(8,128)S(1)} %slice-done.3), channel_id=1, replica_groups=mesh['row'=8,'col'=4] {'col'}, dimensions={2}, use_global_device_ids=true | all-gather | bytes 655360 | tf_op jit(solution)/shard_map/all_gather | solution.py:82
  34.8 1.1 pad_maximum_fusion.3
  35.9 5.2 %pad_maximum_fusion.2 = f32[36,128,256]{2,1,0:T(8,128)} fusion(f32[18,128,256]{2,1,0:T(8,128)} %slice.38, f32[18,128,256]{2,1,0:T(8,128)S(1)} %slice-done.1), kind=kLoop, calls=%fused_computation.6 | loop fusion | flops 1179648 | bytes 9437184 | tf_op jit(solution)/shard_map/concatenate | solution.py:86
  41.0 77.4 %all-reduce.3.cloned.1.call-done = f32[1024,1024]{1,0:T(8,128)} async-done(((f32[1024,1024]{1,0:T(8,128)}), f32[1024,1024]{1,0:T(8,128)}) %all-reduce.3.cloned.1.call-update) | async-done | bytes 4194320 | tf_op jit(solution)/shard_map/psum | solution.py:92
  118.5 3.7 fusion.2
  122.2 3.8 fusion.4
  126.0 126.1 %all-gather.4.cloned.1.call-done.a1.a2 = f32[48,128,1024]{2,1,0:T(8,128)} async-done(((f32[48,128,256]{2,1,0:T(8,128)}), f32[48,128,1024]{2,1,0:T(8,128)}) %all-gather.4.cloned.1.call-update) | async-done | bytes 25165840 | tf_op jit(solution)/shard_map/all_gather | solution.py:82
  252.2 0.5 all-gather.8.cloned.1.call-update
  252.8 4.5 fusion
  257.3 91.5 %all-reduce.5.cloned.1.call-done = f32[1024,1024]{1,0:T(8,128)} async-done(((f32[1024,1024]{1,0:T(8,128)}), f32[1024,1024]{1,0:T(8,128)}) %all-reduce.5.cloned.1.call-update) | async-done | bytes 4194320 | tf_op jit(solution)/shard_map/psum | solution.py:97
  348.8 8.9 %pad_maximum_fusion = f32[2,1024,1024]{2,1,0:T(8,128)} fusion(f32[1,1024,1024]{2,1,0:T(8,128)} %bitcast.23, f32[1,1024,1024]{2,1,0:T(8,128)} %bitcast.22), kind=kLoop, calls=%fused_computation | loop fusion | flops 2097152 | bytes 16777216 | tf_op jit(solution)/shard_map/stack | solution.py:102
  357.8 2.9 fusion.1
  360.7 46.4 %shard_map.59.refs_5_ = f32[46,128,1024]{2,1,0:T(8,128)} custom-call(f32[48,128,1024]{2,1,0:T(8,128)} %all-gather.4.cloned.1.call-done.a1.a2, f32[48,128,1024]{2,1,0:T(8,128)} %all-gather.4.cloned.1.call-done.a1.a2, f32[48,128,1024]{2,1,0:T(8,128)} %refs_0_.5, f32[48,128,1024]{2,1,0:T(8,128)} %refs_0_.5, bf16[1024,1024]{1,0:T(8,128)(2,1)S(1)} %copy-done, ...), custom_call_target="tpu_custom_call" | custom-call | flops 38654705664 | bytes 58720256 | tf_op jit(solution)/shard_map/pallas_call | solution.py:64
  407.1 23.0 %all-gather.8.cloned.1.call-done.a1.a2 = f32[36,128,1024]{2,1,0:T(8,128)} async-done(((f32[36,128,256]{2,1,0:T(8,128)}), f32[36,128,1024]{2,1,0:T(8,128)}) %all-gather.8.cloned.1.call-update) | async-done | bytes 18874384 | tf_op jit(solution)/shard_map/all_gather | solution.py:82
  430.1 1.6 copy-done.1
  431.7 35.5 %shard_map.60.refs_5_ = f32[46,128,1024]{2,1,0:T(8,128)} custom-call(f32[36,128,1024]{2,1,0:T(8,128)} %all-gather.8.cloned.1.call-done.a1.a2, f32[36,128,1024]{2,1,0:T(8,128)} %all-gather.8.cloned.1.call-done.a1.a2, f32[48,128,1024]{2,1,0:T(8,128)} %refs_0_.5, bf16[1024,1024]{1,0:T(8,128)(2,1)S(1)} %copy-done.1, ...), custom_call_target="tpu_custom_call", output_to_operand_aliasing={{}: (7, {})} | custom-call | flops 28991029248 | bytes 46137344 | tf_op jit(solution)/shard_map/pallas_call | solution.py:64
  467.2 17.0 %all-gather.6.cloned.1.call-done.a1.a2 = f32[8,128,1024]{2,1,0:T(8,128)} async-done(((f32[8,128,256]{2,1,0:T(8,128)}), f32[8,128,1024]{2,1,0:T(8,128)}) %all-gather.6.cloned.1.call-update) | async-done | bytes 4194320 | tf_op jit(solution)/shard_map/all_gather | solution.py:82
  484.3 1.6 copy-done.2
  485.8 11.3 %shard_map.61 = f32[46,128,1024]{2,1,0:T(8,128)} custom-call(f32[8,128,1024]{2,1,0:T(8,128)} %all-gather.6.cloned.1.call-done.a1.a2, f32[8,128,1024]{2,1,0:T(8,128)} %all-gather.6.cloned.1.call-done.a1.a2, f32[48,128,1024]{2,1,0:T(8,128)} %refs_0_.5, bf16[1024,1024]{1,0:T(8,128)(2,1)S(1)} %copy-done.2, ...), custom_call_target="tpu_custom_call", output_to_operand_aliasing={{}: (7, {})} | custom-call | flops 6442450944 | bytes 16777216 | tf_op jit(solution)/shard_map/pallas_call | solution.py:64
  (27 shorter events, 0.8 us)
Async XLA Ops:
  8.0 110.5 %all-reduce.3.cloned.1.call-start = ((), (), s32[]{:S(2)}) async-start(), calls=%async_computation | async-start | bytes 8388608 | tf_op jit(solution)/shard_map/psum | solution.py:92
  8.0 1.9 slice-start
  8.1 2.8 slice-start.4
  19.1 233.0 %all-gather.4.cloned.1.call-start = ((), (), s32[]{:S(2)}) async-start(), calls=%async_computation.1 | async-start | bytes 31457280 | tf_op jit(solution)/shard_map/all_gather | solution.py:82
  19.7 329.2 %all-reduce.5.cloned.1.call-start = ((), (), s32[]{:S(2)}) async-start(), calls=%async_computation.2 | async-start | bytes 8388608 | tf_op jit(solution)/shard_map/psum | solution.py:97
  19.7 3.6 slice-start.3
  19.7 15.0 %slice-start.2 = ((f32[47,128,256]{2,1,0:T(8,128)}), f32[4,128,256]{2,1,0:T(8,128)S(1)}, s32[]{:S(2)}) async-start(f32[47,128,256]{2,1,0:T(8,128)} %param.5), calls=%async_computation.7 | async-start | bytes 1048576 | tf_op jit(solution)/shard_map/slice | solution.py:86
  19.7 15.0 %slice-start.5 = ((f32[46,128,256]{2,1,0:T(8,128)}), f32[4,128,256]{2,1,0:T(8,128)S(1)}, s32[]{:S(2)}) async-start(f32[46,128,256]{2,1,0:T(8,128)} %param.6), calls=%async_computation.10 | async-start | bytes 1048576 | tf_op jit(solution)/shard_map/slice | solution.py:86
  19.8 16.1 %slice-start.1 = ((f32[47,128,256]{2,1,0:T(8,128)}), f32[18,128,256]{2,1,0:T(8,128)S(1)}, s32[]{:S(2)}) async-start(f32[47,128,256]{2,1,0:T(8,128)} %param.5), calls=%async_computation.6 | async-start | bytes 4718592 | tf_op jit(solution)/shard_map/slice | solution.py:86
  41.0 81.1 %copy-start.4 = (f32[2,1024,128]{2,1,0:T(8,128)S(1)}, f32[2,1024,128]{2,1,0:T(8,128)}, u32[]{:S(2)}) copy-start(f32[2,1024,128]{2,1,0:T(8,128)} %param.7) | copy-start | bytes 3145732
  252.1 178.0 %all-gather.8.cloned.1.call-start = ((), (), s32[]{:S(2)}) async-start(), calls=%async_computation.4 | async-start | bytes 23592960 | tf_op jit(solution)/shard_map/all_gather | solution.py:82
  252.7 231.5 %all-gather.6.cloned.1.call-start = ((), (), s32[]{:S(2)}) async-start(), calls=%async_computation.3 | async-start | bytes 5242880 | tf_op jit(solution)/shard_map/all_gather | solution.py:82
  348.8 8.9 %copy-start.3 = (f32[1024,1024]{1,0:T(8,128)S(1)}, f32[1024,1024]{1,0:T(8,128)}, u32[]{:S(2)}) copy-start(f32[1024,1024]{1,0:T(8,128)} %all-reduce.5.cloned.1.call-done) | copy-start | bytes 12582916
  357.8 2.9 copy-start
  430.1 1.6 copy-start.1
  484.2 1.6 copy-start.2
Sparse Core Ops, SparseCore 0:
  19.2 99.2 all-reduce.2
  252.3 96.5 all-reduce.4
Sparse Core Ops, SparseCore 1:
  22.0 230.1 all-gather.3
  254.5 175.6 all-gather.7
  431.8 52.4 all-gather.5
